TPU v7x, 512 devices: a whole 4x8x8 slice. The times are simulated.
512 devices in a mesh: grid: 64 (over x, z, core), mesh: 8 (over y).
Axes of the slice: x: 4, y: 8, z: 8, core: 2. Of those that a mesh axis runs over, the one named last changes fastest.
Arguments:
- grid_features: bfloat16 [474, 131072], P(None, ('grid', 'mesh')), may hold values from -6 to 6
- edge_feats: float32 [4, 262144], P(None, ('grid', 'mesh')), may hold values from -6 to 6
- edge_src: int32 [262144], P(('grid', 'mesh')), may hold values from 0 to 255, as said below
- edge_dst: int32 [262144], P(('grid', 'mesh')), may hold values from 0 to 65535, as said below
- edge_count: int32 [512], P(('grid', 'mesh')), may hold values from 16 to 512, as said below
- mesh_lat: bfloat16 [65536, 512], P(('grid', 'mesh')), may hold values from -6 to 6
- owner_map: int32 [65536], P(('grid', 'mesh')), may hold values from 0 to 65535, as said below
- w_grid: bfloat16 [474, 512], replicated, may hold values from -0.25 to 0.25
- w_edge: float32 [4, 512], replicated, may hold values from -3 to 3
- w_msg_in: bfloat16 [1024, 512], replicated, may hold values from -0.1875 to 0.1875
- w_msg_out: bfloat16 [512, 512], replicated, may hold values from -0.25 to 0.25
- gain_msg: float32 [512], replicated, may hold values from 0.5 to 1.5
- w_node_in: bfloat16 [1024, 512], replicated, may hold values from -0.1875 to 0.1875
- w_node_out: bfloat16 [512, 512], replicated, may hold values from -0.25 to 0.25
- gain_node: float32 [512], replicated, may hold values from 0.5 to 1.5
Outputs:
- mesh_out: bfloat16 [65536, 512], P(('grid', 'mesh'))
Inputs may be any that keep to these rules, and one draw needn't show every extreme that they name: `edge_src`: index among the 256 grid nodes of the device that holds the edge; 0 on slots that are not live. `edge_dst`: live slots of a device come first and are sorted by destination, and every destination lies on an owner with the device's own mesh index; slots that are not live hold 0. From one device, at most 16 live edges go to one owner and they reach at most 4 distinct positions; for each mesh index one owner receives exactly 16 live edges over exactly 4 positions from every device of that mesh index. `edge_count`: number of live slots of each device; in every draw some device has all 512 slots live. `owner_map`: A permutation; the positions of an aligned block of 8 * 128 positions (one grid index) hold the nodes of the same block, and each owner holds exactly 128 / 8 nodes of each device of its grid index.
All inputs are finite; a program needn't handle non-finite values.
Results may differ from a plain program's by a relative error of at most 0.005.
Values may be sent and summed in bfloat16 or wider, within the bound.
A program may use at most 64 MiB of HBM per device.

v0:
```python
import jax
import jax.numpy as jnp
from jax import lax
from jax.sharding import PartitionSpec as P


def layer_norm(values, scaling):
    row_mean = jnp.mean(values, axis=-1, keepdims=True)
    centred = values - row_mean
    variance = jnp.mean(centred * centred, axis=-1, keepdims=True)
    return centred * lax.rsqrt(variance + 1e-05) * scaling


def edge_messages(
    features, edge_part, sources, live_count, w_grid, w_edge, w_msg_in, w_msg_out, gain_msg
):
    grid_latent = jax.nn.silu(
        lax.dot_general(
            features, w_grid, (((0,), (0,)), ((), ())), preferred_element_type=jnp.float32
        )
    ).astype(jnp.bfloat16)
    edge_latent = jax.nn.silu(
        lax.dot_general(
            edge_part,
            w_edge,
            (((0,), (0,)), ((), ())),
            precision=lax.Precision.HIGHEST,
            preferred_element_type=jnp.float32,
        )
    ).astype(jnp.bfloat16)
    sender_latent = jnp.take(grid_latent, sources, axis=0)
    latent_width = w_msg_out.shape[0]
    preactivation = jnp.dot(
        edge_latent, w_msg_in[:latent_width], preferred_element_type=jnp.float32
    ) + jnp.dot(sender_latent, w_msg_in[latent_width:], preferred_element_type=jnp.float32)
    hidden_edge = jax.nn.silu(preactivation).astype(jnp.bfloat16)
    mixed = jnp.dot(hidden_edge, w_msg_out, preferred_element_type=jnp.float32)
    is_live = jnp.arange(sources.shape[0], dtype=jnp.int32) < live_count
    renewed = edge_latent.astype(jnp.float32) + layer_norm(mixed, gain_msg)
    return jnp.where(is_live[:, None], renewed, jnp.zeros_like(renewed)).astype(jnp.bfloat16)


def shards(
    grid_features,
    edge_feats,
    edge_src,
    edge_dst,
    edge_count,
    mesh_lat,
    owner_map,
    w_grid,
    w_edge,
    w_msg_in,
    w_msg_out,
    gain_msg,
    w_node_in,
    w_node_out,
    gain_node,
):
    live_count = edge_count[0]
    message = edge_messages(
        grid_features,
        edge_feats,
        edge_src,
        live_count,
        w_grid,
        w_edge,
        w_msg_in,
        w_msg_out,
        gain_msg,
    )
    groups = lax.axis_size("grid")
    columns = lax.axis_size("mesh")
    nodes_dev = mesh_lat.shape[0]
    slot_count = edge_src.shape[0]
    is_live = jnp.arange(slot_count, dtype=jnp.int32) < live_count
    owner_grid = jnp.where(is_live, edge_dst // (nodes_dev * columns), groups)
    local_node = edge_dst % nodes_dev
    membership = jnp.arange(groups, dtype=jnp.int32)[:, None] == owner_grid[None, :]
    capacity = 2 * slot_count // groups
    per_owner = jnp.sum(membership.astype(jnp.int32), axis=1)
    owner_start = jnp.cumsum(per_owner) - per_owner
    offsets = jnp.arange(capacity, dtype=jnp.int32)
    slot_valid = (offsets[None, :] < per_owner[:, None]).reshape(-1)
    source_row = jnp.where(slot_valid, (owner_start[:, None] + offsets[None, :]).reshape(-1), 0)
    packed = jnp.where(
        slot_valid[:, None], jnp.take(message, source_row, axis=0), jnp.zeros((), jnp.bfloat16)
    )
    target_node = jnp.where(slot_valid, jnp.take(local_node, source_row), 0)
    arrived, arrived_target = (
        lax.all_to_all(packed, "grid", split_axis=0, concat_axis=0, tiled=True),
        lax.all_to_all(target_node, "grid", split_axis=0, concat_axis=0, tiled=True),
    )
    placing = (jnp.arange(nodes_dev, dtype=jnp.int32)[:, None] == arrived_target[None, :]).astype(
        jnp.bfloat16
    )
    gathered = jnp.dot(placing, arrived, preferred_element_type=jnp.float32)
    summed_low = gathered.astype(jnp.bfloat16)
    latent_width = w_node_out.shape[0]
    preactivation = jnp.dot(
        mesh_lat, w_node_in[:latent_width], preferred_element_type=jnp.float32
    ) + jnp.dot(summed_low, w_node_in[latent_width:], preferred_element_type=jnp.float32)
    hidden_node = jax.nn.silu(preactivation).astype(jnp.bfloat16)
    mixed = jnp.dot(hidden_node, w_node_out, preferred_element_type=jnp.float32)
    renewed = (mesh_lat.astype(jnp.float32) + layer_norm(mixed, gain_node)).astype(jnp.bfloat16)
    every_row, every_id = (
        lax.all_gather(renewed, "mesh", axis=0, tiled=True),
        lax.all_gather(owner_map, "mesh", axis=0, tiled=True),
    )
    first_node = (lax.axis_index("grid") * columns + lax.axis_index("mesh")) * nodes_dev
    wanted = jnp.arange(nodes_dev, dtype=jnp.int32) + first_node
    placing_rows = (wanted[:, None] == every_id[None, :]).astype(jnp.bfloat16)
    return jnp.dot(placing_rows, every_row, preferred_element_type=jnp.float32).astype(jnp.bfloat16)


def solution(mesh):
    placed = (
        P(None, ("grid", "mesh")),
        P(None, ("grid", "mesh")),
        P(("grid", "mesh")),
        P(("grid", "mesh")),
        P(("grid", "mesh")),
        P(("grid", "mesh"), None),
        P(("grid", "mesh")),
        P(),
        P(),
        P(),
        P(),
        P(),
        P(),
        P(),
        P(),
    )
    return jax.shard_map(
        shards, mesh=mesh, in_specs=placed, out_specs=P(("grid", "mesh"), None), check_vma=False
    )
```

profile of v0, /device:TPU:4, one launch (start us, length us, event | category | flops | bytes accessed | tf_op | source)
XLA Modules:
  0.0 134.3 jit_solution(18142507474107245675)
XLA Ops:
  7.9 6.9 %gather_fusion = s32[1024]{0:T(1024)S(1)} fusion(s32[512]{0:T(512)S(1)} %get-tuple-element.5, s32[1024]{0:T(1024)S(1)} %broadcast_clamp_fusion), kind=kCustom, calls=%fused_computation | custom fusion | bytes 12288 | tf_op jit(solution)/shard_map/jit(_take)/gather | solution.py:89
  14.9 0.7 select_select_fusion.1
  15.6 14.1 %all-to-all-start = ((s32[64,16,1]{1,2,0:T(1,128)}), s32[64,16,1]{1,2,0:T(1,128)S(1)}, u32[]{:S(2)}, u32[]{:S(2)}) async-start(s32[64,16,1]{1,2,0:T(1,128)} %bitcast.5), calls=%async_computation | async-start | bytes 65536 | tf_op jit(solution)/shard_map/all_to_all | solution.py:92
  29.8 0.6 copy-done.12
  30.4 1.2 multiply_convert_fusion.1
  31.7 0.4 fusion.6
  32.1 0.6 copy-done.10
  32.7 0.4 multiply_convert_fusion.2
  33.1 2.6 %gather_fusion.1 = bf16[512,512]{1,0:T(8,128)(2,1)} fusion(bf16[256,512]{1,0:T(8,128)(2,1)S(1)} %multiply_convert_fusion.2, s32[1024]{0:T(1024)S(1)} %pad_clamp_fusion), kind=kCustom, calls=%fused_computation.1 | custom fusion | bytes 1050624 | tf_op jit(solution)/shard_map/jit(_take)/gather | solution.py:31
  35.8 2.3 %fusion.31 = (f32[512]{0:T(512)S(1)}, f32[512,512]{0,1:T(8,128)S(1)}) fusion(bf16[512,512]{1,0:T(8,128)(2,1)S(1)} %copy-done, f32[512,512]{1,0:T(8,128)S(1)} %fusion.6, bf16[1024,512]{1,0:T(8,128)(2,1)} %param.24, bf16[512,512]{1,0:T(8,128)(2,1)} %gather_fusion.1, pred[512]{0:T(512)(128)(4,1)S(1)} %compare_and_fusion.1), kind=kOutput, calls=%fused_computation.67 | convolution fusion | flops 538967552 | bytes 3672576 | tf_op jit(solution)/shard_map/dot_general | solution.py:37
  38.7 0.7 copy-done.8
  39.7 4.0 %gather_fusion.2 = bf16[1024,512]{1,0:T(8,128)(2,1)S(1)} fusion(bf16[512,512]{1,0:T(8,128)(2,1)S(1)} %select_convert_fusion, s32[1024]{0:T(1024)S(1)} %broadcast_clamp_fusion), kind=kCustom, calls=%fused_computation.2 | custom fusion | bytes 2101248 | tf_op jit(solution)/shard_map/jit(_take)/gather | solution.py:87
  43.6 1.2 select_select_fusion
  44.9 10.5 %all-to-all-start.1 = ((bf16[64,16,512]{2,1,0:T(8,128)(2,1)}), bf16[64,16,512]{2,1,0:T(8,128)(2,1)S(1)}, u32[]{:S(2)}, u32[]{:S(2)}) async-start(bf16[64,16,512]{2,1,0:T(8,128)(2,1)} %select_select_fusion), calls=%async_computation.1 | async-start | bytes 2097152 | tf_op jit(solution)/shard_map/all_to_all | solution.py:91
  55.6 0.5 broadcast.258
  56.2 0.7 reduce.4
  57.0 25.0 %all-to-all-done.1 = bf16[64,16,512]{2,1,0:T(8,128)(2,1)S(1)} async-done(((bf16[64,16,512]{2,1,0:T(8,128)(2,1)}), bf16[64,16,512]{2,1,0:T(8,128)(2,1)S(1)}, u32[]{:S(2)}, u32[]{:S(2)}) %all-to-all-start.1) | async-done | bytes 1048608 | tf_op jit(solution)/shard_map/all_to_all | solution.py:91
  82.0 1.2 multiply_convert_fusion.3
  83.2 1.2 fusion.36
  84.6 0.8 add_convert_fusion
  85.5 0.6 copy-done.9
  86.1 16.6 %all-gather = s32[8,1,128]{2,1,0:T(1,128)S(1)} all-gather(s32[1,1,128]{2,1,0:T(1,128)S(1)} %bitcast.27), channel_id=1, replica_groups=mesh['grid'=64,'mesh'=8] {'mesh'}, dimensions={0}, use_global_device_ids=true | all-gather | bytes 4608 | tf_op jit(solution)/shard_map/all_gather | solution.py:108
  102.8 22.5 %all-gather.3.cloned.1.call-done = bf16[1024,512]{1,0:T(8,128)(2,1)} async-done(((bf16[128,512]{1,0:T(8,128)(2,1)}), bf16[1024,512]{1,0:T(8,128)(2,1)}) %all-gather.3.cloned.1.call-update) | async-done | bytes 1048592 | tf_op jit(solution)/shard_map/all_gather | solution.py:107
  125.3 2.2 %convolution_convert_fusion = bf16[128,512]{1,0:T(8,128)(2,1)} fusion(bf16[1024,512]{1,0:T(8,128)(2,1)} %all-gather.3.cloned.1.call-done, s32[1024]{0:T(1024)S(1)} %bitcast.24, s32[128]{0:T(128)S(1)} %iota_add_fusion), kind=kOutput, calls=%fused_computation.5 | convolution fusion | flops 134414336 | bytes 1184256 | tf_op jit(solution)/shard_map/dot_general | solution.py:113
  (54 shorter events, 2.4 us)
Async XLA Ops:
  6.5 29.2 %copy-start = (bf16[512,512]{1,0:T(8,128)(2,1)S(1)}, bf16[512,512]{1,0:T(8,128)(2,1)}, u32[]{:S(2)}) copy-start(bf16[512,512]{1,0:T(8,128)(2,1)} %param.25) | copy-start | bytes 1572868
  6.5 0.7 copy-start.7
  15.6 14.1 %copy-start.5 = (s32[512]{0:T(512)S(1)}, s32[512]{0:T(512)}, u32[]{:S(2)}) copy-start(s32[512]{0:T(512)} %param.17) | copy-start | bytes 6148
  15.6 29.3 %all-to-all-start = ((s32[64,16,1]{1,2,0:T(1,128)}), s32[64,16,1]{1,2,0:T(1,128)S(1)}, u32[]{:S(2)}, u32[]{:S(2)}) async-start(s32[64,16,1]{1,2,0:T(1,128)} %bitcast.5), calls=%async_computation | async-start | bytes 65536 | tf_op jit(solution)/shard_map/all_to_all | solution.py:92
  29.7 0.7 copy-start.12
  29.7 0.7 copy-start.13
  30.4 1.2 copy-start.4
  31.6 1.0 copy-start.10
  31.7 1.1 copy-start.11
  38.7 0.7 copy-start.8
  44.9 10.5 %copy-start.2 = (bf16[128,512]{1,0:T(8,128)(2,1)S(1)}, bf16[128,512]{1,0:T(8,128)(2,1)}, u32[]{:S(2)}) copy-start(bf16[128,512]{1,0:T(8,128)(2,1)} %param.20) | copy-start | bytes 393220
  44.9 10.5 %copy-start.3 = (bf16[1024,512]{1,0:T(8,128)(2,1)S(1)}, bf16[1024,512]{1,0:T(8,128)(2,1)}, u32[]{:S(2)}) copy-start(bf16[1024,512]{1,0:T(8,128)(2,1)} %param.27) | copy-start | bytes 3145732
  44.9 37.1 %all-to-all-start.1 = ((bf16[64,16,512]{2,1,0:T(8,128)(2,1)}), bf16[64,16,512]{2,1,0:T(8,128)(2,1)S(1)}, u32[]{:S(2)}, u32[]{:S(2)}) async-start(bf16[64,16,512]{2,1,0:T(8,128)(2,1)} %select_select_fusion), calls=%async_computation.1 | async-start | bytes 2097152 | tf_op jit(solution)/shard_map/all_to_all | solution.py:91
  55.3 69.9 %all-gather.3.cloned.1.call-start = ((), (), s32[]{:S(2)}) async-start(), calls=%async_computation.2 | async-start | bytes 1179648 | tf_op jit(solution)/shard_map/all_gather | solution.py:107
  82.0 1.2 copy-start.1
  83.2 1.4 %copy-start.6 = (f32[512]{0:T(512)S(1)}, f32[512]{0:T(512)}, u32[]{:S(2)}) copy-start(f32[512]{0:T(512)} %param.29) | copy-start | bytes 6148
  85.5 0.7 copy-start.9
Sparse Core Ops, SparseCore 0:
  85.6 39.6 all-gather.2
where the time goes:
time: 135 us; the launch traced here: 134 us
  waiting for transfers between devices  47.6 us (35%)
  starting transfers between devices  24.6 us (18%)
  local copies, waits for them, and re-layouts  17.3 us (13%)
  blocking collectives  16.6 us (12%)
  between operations  14.4 us (11%)
  matrix products  9.15 us (7%)
  other arithmetic  4.77 us (4%)
    all_to_all x1, waiting for transfers between devices, shards(): lax.all_to_all(packed, 'grid', split_axis=0, concat_axis=0, tiled=True)  25 us
    all_gather x1, waiting for transfers between devices, shards(): lax.all_gather(renewed, 'mesh', axis=0, tiled=True)  22.5 us
    all_gather x1, blocking collectives, shards(): lax.all_gather(owner_map, 'mesh', axis=0, tiled=True)  16.6 us
    all_to_all x1, starting transfers between devices, shards(): lax.all_to_all(target_node, 'grid', split_axis=0, concat_axis=0, tiled=True)  14.1 us
    all_to_all x1, starting transfers between devices, shards(): lax.all_to_all(packed, 'grid', split_axis=0, concat_axis=0, tiled=True)  10.5 us
    gather x2, local copies, waits for them, and re-layouts, shards(): target_node = jnp.where(slot_valid, jnp.take(local_node, source_row), 0)  6.94 us
    gather x1, local copies, waits for them, and re-layouts, shards(): jnp.take(message, source_row, axis=0)  3.97 us
  transfers between devices with their start and end apart: 3, of which 2 were waited for; matrix products, arithmetic and copies ran while one was open for 11% of the time, Pallas kernels for 0%

commit v1 on v0

v1 whole, which is shorter than its diff:
```python
import functools

import jax
import jax.numpy as jnp
from jax import lax
from jax.experimental import pallas as pl
from jax.experimental.pallas import tpu as pltpu
from jax.sharding import PartitionSpec as P

F32 = jnp.float32
BF16 = jnp.bfloat16
MESH = pl.DeviceIdType.MESH
CAP = 4
TILE = 16
LOG_CORES = 1
LOG_RING = 3
CORES = 1 << LOG_CORES
RING = 1 << LOG_RING


def far_first(size):
    return sorted(range(1, size), key=lambda step: -min(step, size - step))


def silu(v):
    half = 0.5 * v
    return half + half * jnp.tanh(half)


def normed(v):
    mean = jnp.mean(v, axis=-1, keepdims=True)
    centred = v - mean
    variance = jnp.mean(centred * centred, axis=-1, keepdims=True)
    return centred * lax.rsqrt(variance + 1e-05)


def dot(a, b):
    return lax.dot_general(a, b, (((1,), (0,)), ((), ())), preferred_element_type=F32)


def dot_tn(a, b):
    return lax.dot_general(a, b, (((0,), (0,)), ((), ())), preferred_element_type=F32)


def dot_nt(a, b):
    return lax.dot_general(a, b, (((1,), (1,)), ((), ())), preferred_element_type=F32)


def iota(shape, dim):
    return lax.broadcasted_iota(jnp.int32, shape, dim)


def hot(mask):
    return jnp.where(mask, 1.0, 0.0).astype(BF16)


def parts(v):
    a = v.astype(BF16).astype(F32)
    rest = v - a
    b = rest.astype(BF16).astype(F32)
    return a, b, rest - b


def kernel(
    groups,
    columns,
    feat_h,
    ef_h,
    src_h,
    dst_h,
    lat_h,
    map_h,
    w_grid_h,
    w_edge_h,
    w_mi_h,
    w_mo_h,
    gain_m_h,
    w_ni_h,
    w_no_h,
    gain_n_h,
    out_ref,
    feat,
    ef,
    src,
    dst,
    lat,
    omap,
    w_grid,
    w_edge,
    w_mi,
    w_mo,
    gain_m,
    w_ni,
    w_no,
    gain_n,
    message,
    wide,
    send,
    recv,
    id_send,
    id_passed,
    id_recv,
    adding,
    place_send,
    place_recv,
    row_send,
    row_recv,
    load_sem,
    id_sems,
    id_sems_2,
    place_sems,
    pay_sems,
    row_sems,
):
    width = w_mo.shape[0]
    slots = dst.shape[1]
    nodes = omap.shape[1]
    g_nodes = feat.shape[1]
    me = lax.axis_index("grid")
    my = lax.axis_index("mesh")

    loads = {}
    pairs = (
        (dst_h, dst),
        (src_h, src),
        (ef_h, ef),
        (w_edge_h, w_edge),
        (feat_h, feat),
        (w_grid_h, w_grid),
        (w_mi_h, w_mi),
        (w_mo_h, w_mo),
        (gain_m_h, gain_m),
        (map_h, omap),
        (lat_h, lat),
        (w_ni_h, w_ni),
        (w_no_h, w_no),
        (gain_n_h, gain_n),
    )
    for at, (here, there) in enumerate(pairs):
        loads[id(there)] = pltpu.make_async_copy(here, there, load_sem.at[at])
    for there in (dst, omap, src, ef, w_edge, feat, w_grid, w_mi, w_mo, gain_m):
        loads[id(there)].start()

    def ready(*refs):
        for ref in refs:
            loads[id(ref)].wait()

    depth = groups // CORES // RING
    spokes = depth * CORES
    core = lax.rem(me, CORES)
    ring_at = lax.rem(lax.div(me, CORES), RING)
    spoke_at = lax.div(me, CORES * RING) * CORES + core

    def ring_peer(step):
        at = lax.rem(ring_at + step, RING)
        return at, me + (at - ring_at) * CORES

    def spoke_peer(step):
        at = lax.rem(spoke_at + step, spokes)
        return at, (lax.div(at, CORES) * RING + ring_at) * CORES + lax.rem(at, CORES)

    ring_steps = far_first(RING)
    spoke_steps = far_first(spokes)
    mesh_steps = far_first(columns)
    barrier = pltpu.get_barrier_semaphore()

    def ring_turn(turn):
        step = lax.div(RING - turn, 2) * (1 - 2 * lax.rem(turn, 2))
        return lax.rem(ring_at + step + RING, RING)

    def greet(peer):
        pl.semaphore_signal(barrier, inc=1, device_id={"grid": peer}, device_id_type=MESH)

    def greet_ring(turn, carry):
        at = ring_turn(turn)
        for spoke in range(spokes):
            greet((spoke // CORES * RING + at) * CORES + spoke % CORES)
        return carry

    lax.fori_loop(0, RING - 1, greet_ring, 0)
    for step in spoke_steps:
        greet(spoke_peer(step)[1])
    for step in mesh_steps:
        to = {"mesh": lax.rem(my + step, columns)}
        pl.semaphore_signal(barrier, inc=1, device_id=to, device_id_type=MESH)

    shift = (nodes * columns).bit_length() - 1
    upto = hot(iota((slots, slots), 0) <= iota((slots, slots), 1))
    ready(dst, omap, src, ef, w_edge)
    target = jnp.broadcast_to(dst[...], (8, slots))
    edge_at = iota((8, slots), 1)
    last = jnp.max(jnp.where(target > 0, edge_at, -1), axis=1, keepdims=True)
    live = edge_at <= last
    fresh = live & ((edge_at == 0) | (target != pltpu.roll(target, 1, 1)))
    fresh_f = jnp.where(fresh, 1.0, 0.0)
    band = lax.shift_right_logical(target, shift)
    low = band & (CORES - 1)
    along = lax.shift_right_logical(band, LOG_CORES) & (RING - 1)
    across = lax.shift_right_logical(band, LOG_CORES + LOG_RING)
    owner = jnp.where(live, along * spokes + across * CORES + low, -1)
    of_owner = owner[0:1] == iota((groups, slots), 0)
    counted = dot(jnp.where(of_owner, fresh_f[0:1], 0.0).astype(BF16), upto)
    rank = jnp.sum(jnp.where(of_owner, counted, 0.0), axis=0, keepdims=True)
    row_of_edge = jnp.where(
        live[0:1], (rank.astype(jnp.int32) - 1) * groups + owner[0:1], -1
    )
    picking = hot(row_of_edge == iota((CAP * groups, slots), 0))
    local_f = jnp.where(fresh, (target & (nodes - 1)).astype(F32), 0.0)
    ids = dot_nt(picking, jnp.broadcast_to(local_f[0:1], (128, slots)).astype(BF16))
    lane = iota((groups, 128), 1)
    keys = ids[0:groups]
    for j in range(1, CAP):
        keys = jnp.where(lane & (CAP - 1) == j, ids[j * groups : (j + 1) * groups], keys)
    id_send[...] = keys.reshape(RING, spokes, 1, 128)

    share = nodes // columns
    node_shift = nodes.bit_length() - 1
    held = omap[...]
    home = lax.shift_right_logical(held, node_shift) & (columns - 1)
    at_home = home == iota((columns, nodes), 0)
    before = hot(iota((nodes, nodes), 0) <= iota((nodes, nodes), 1))
    nth = dot(hot(at_home), before)
    leave = jnp.sum(
        jnp.where(at_home, nth + (iota((columns, nodes), 0) * share - 1).astype(F32), 0.0),
        axis=0,
        keepdims=True,
    )
    leaving = hot(leave.astype(jnp.int32) == iota((nodes, nodes), 0))
    node_hot_t = hot((held & (nodes - 1)) == iota((nodes, nodes), 0))
    place_send[...] = dot_nt(leaving, node_hot_t).astype(BF16)
    position = dot_nt(
        leaving, jnp.broadcast_to(iota((1, nodes), 1).astype(F32), (128, nodes)).astype(BF16)
    )

    ready(feat, w_grid)
    e1, e2, e3 = parts(ef[...])
    w1, w2, w3 = parts(w_edge[...])
    e_all = jnp.concatenate([e1, e1, e2, e1, e2, e3], axis=0).astype(BF16)
    w_all = jnp.concatenate([w1, w2, w1, w3, w2, w1], axis=0).astype(BF16)
    edge_latent = silu(dot_tn(e_all, w_all)).astype(BF16)
    grid_latent = silu(dot_tn(feat[...], w_grid[...])).astype(BF16)
    from_node = jnp.transpose(jnp.broadcast_to(src[...], (128, slots)))
    gathering = [hot(from_node == iota((slots, 128), 1) + at) for at in range(0, g_nodes, 128)]
    ready(w_mi)
    w_mi[width : width + g_nodes] = dot(grid_latent, w_mi[width:]).astype(BF16)
    both = jnp.concatenate([edge_latent] + gathering, axis=1)
    hidden = silu(dot(both, w_mi[0 : width + g_nodes])).astype(BF16)
    ready(w_mo, gain_m)
    for there in (lat, w_ni, w_no, gain_n):
        loads[id(there)].start()
    mixed = dot(hidden, w_mo[...])
    message[...] = (edge_latent.astype(F32) + normed(mixed) * gain_m[...]).astype(BF16)
    summed = dot(picking, message[...])
    quarters = width // 128
    for j in range(CAP):
        for c in range(quarters):
            wide[pl.ds(j * quarters + c, groups, stride=TILE), :] = summed[
                j * groups : (j + 1) * groups, c * 128 : (c + 1) * 128
            ]
    send[...] = wide[...].astype(BF16).reshape(groups, TILE, 128)
    pl.semaphore_wait(barrier, groups + columns - 2)

    def remote(outgoing, incoming, sems, to):
        return pltpu.make_async_remote_copy(
            src_ref=outgoing,
            dst_ref=incoming,
            send_sem=sems.at[0],
            recv_sem=sems.at[1],
            device_id=to,
            device_id_type=MESH,
        )

    def along_ring(outgoing, incoming, sems):
        for step in ring_steps:
            at, peer = ring_peer(step)
            remote(outgoing.at[at], incoming.at[ring_at], sems, {"grid": peer}).start()
        incoming[pl.ds(ring_at, 1)] = outgoing[pl.ds(ring_at, 1)]

    def along_spokes(outgoing, incoming, sems):
        for step in spoke_steps:
            at, peer = spoke_peer(step)
            remote(outgoing.at[:, at], incoming.at[spoke_at], sems, {"grid": peer}).start()
        kept = outgoing[:, pl.ds(spoke_at, 1)]
        incoming[pl.ds(spoke_at, 1)] = kept.reshape((1, RING) + kept.shape[2:])

    def along_mesh(outgoing, incoming, sems):
        def rows(at):
            return pl.ds(pl.multiple_of(at * share, share), share)

        for step in mesh_steps:
            peer = lax.rem(my + step, columns)
            remote(outgoing.at[rows(peer)], incoming.at[rows(my)], sems, {"mesh": peer}).start()
        incoming[rows(my), :] = outgoing[rows(my), :]

    def drain(sem, ref):
        pltpu.make_async_copy(ref, ref, sem).wait()

    slot = spoke_at * RING + ring_at

    along_ring(id_send, id_passed, id_sems)

    def pay_ring(turn, carry):
        at = ring_turn(turn)
        for spoke_step in range(spokes):
            spoke = lax.rem(spoke_at + spoke_step, spokes)
            peer = (lax.div(spoke, CORES) * RING + at) * CORES + lax.rem(spoke, CORES)
            block = send.at[at * spokes + spoke]
            remote(block, recv.at[slot], pay_sems, {"grid": peer}).start()
        return carry

    lax.fori_loop(0, RING - 1, pay_ring, 0)
    for step in spoke_steps:
        at, peer = spoke_peer(step)
        block = send.at[ring_at * spokes + at]
        remote(block, recv.at[slot], pay_sems, {"grid": peer}).start()
    recv[pl.ds(slot, 1)] = send[pl.ds(ring_at * spokes + spoke_at, 1)]
    drain(id_sems.at[1], id_passed.at[pl.ds(0, RING - 1)])
    along_spokes(id_passed, id_recv, id_sems_2)

    along_mesh(place_send, place_recv, place_sems)

    ready(lat, w_ni)
    lat_rows = dot(leaving, lat[...])
    pre = dot(lat_rows.astype(BF16), w_ni[0:width])
    drain(id_sems_2.at[1], id_recv.at[pl.ds(0, spokes - 1)])
    lines = id_recv[...].reshape(groups, 128)
    senders = 128 // CAP
    mine = lax.shift_right_logical(iota((senders, 128), 1), CAP.bit_length() - 1) == iota(
        (senders, 128), 0
    )
    for b in range(groups // senders):
        key = jnp.sum(
            jnp.where(mine, lines[b * senders : (b + 1) * senders], 0.0), axis=0, keepdims=True
        )
        adding[:, b * 128 : (b + 1) * 128] = hot(key == position)
    drain(place_sems.at[1], place_recv.at[pl.ds(0, nodes - share)])
    placing = jnp.transpose(place_recv[...].astype(F32)).astype(BF16)
    ready(w_no, gain_n)

    drain(pay_sems.at[1], recv.at[pl.ds(0, groups - 1)])
    wide[...] = recv[...].reshape(groups * TILE, 128).astype(F32)
    rows = jnp.concatenate(
        [wide[pl.ds(c, CAP * groups, stride=quarters), :].astype(BF16) for c in range(quarters)],
        axis=1,
    )
    summed_low = dot(adding[...], rows).astype(BF16)
    hidden_node = silu(pre + dot(summed_low, w_ni[width:])).astype(BF16)
    mixed_node = dot(hidden_node, w_no[...])
    row_send[...] = (lat_rows + normed(mixed_node) * gain_n[...]).astype(BF16)

    along_mesh(row_send, row_recv, row_sems)
    drain(id_sems.at[0], id_send.at[pl.ds(0, RING - 1)])
    drain(id_sems_2.at[0], id_recv.at[pl.ds(0, spokes - 1)])
    drain(place_sems.at[0], place_send.at[pl.ds(0, nodes - share)])
    drain(pay_sems.at[0], send.at[pl.ds(0, groups - 1)])
    drain(row_sems.at[1], row_recv.at[pl.ds(0, nodes - share)])
    out_ref[...] = dot(placing, row_recv[...]).astype(BF16)
    drain(row_sems.at[0], row_send.at[pl.ds(0, nodes - share)])


def shards(
    grid_features,
    edge_feats,
    edge_src,
    edge_dst,
    edge_count,
    mesh_lat,
    owner_map,
    w_grid,
    w_edge,
    w_msg_in,
    w_msg_out,
    gain_msg,
    w_node_in,
    w_node_out,
    gain_node,
):
    groups, columns = lax.axis_size("grid"), lax.axis_size("mesh")
    nodes, width = mesh_lat.shape
    operands = (
        grid_features,
        edge_feats,
        edge_src.reshape(1, -1),
        edge_dst.reshape(1, -1),
        mesh_lat,
        owner_map.reshape(1, -1),
        w_grid,
        w_edge,
        w_msg_in,
        w_msg_out,
        gain_msg.reshape(1, -1),
        w_node_in,
        w_node_out,
        gain_node.reshape(1, -1),
    )
    copies = [pltpu.VMEM(v.shape, v.dtype) for v in operands]
    rows = groups * TILE
    spokes = groups // RING
    return pl.pallas_call(
        functools.partial(kernel, groups, columns),
        out_shape=pltpu.VMEM((nodes, width), BF16),
        in_specs=[pl.BlockSpec(memory_space=pl.ANY)] * len(operands),
        out_specs=pl.BlockSpec(memory_space=pltpu.VMEM),
        scratch_shapes=copies
        + [
            pltpu.VMEM((edge_dst.shape[0], width), BF16),
            pltpu.VMEM((rows, 128), F32),
            pltpu.VMEM((groups, TILE, 128), BF16),
            pltpu.VMEM((groups, TILE, 128), BF16),
            pltpu.VMEM((RING, spokes, 1, 128), F32),
            pltpu.VMEM((RING, spokes, 1, 128), F32),
            pltpu.VMEM((spokes, RING, 1, 128), F32),
            pltpu.VMEM((nodes, CAP * groups), BF16),
            pltpu.VMEM((nodes, nodes), BF16),
            pltpu.VMEM((nodes, nodes), BF16),
            pltpu.VMEM((nodes, width), BF16),
            pltpu.VMEM((nodes, width), BF16),
            pltpu.SemaphoreType.DMA((len(operands),)),
        ]
        + [pltpu.SemaphoreType.DMA((2,))] * 5,
        compiler_params=pltpu.CompilerParams(
            collective_id=0, has_side_effects=True, vmem_limit_bytes=56 * 1024 * 1024
        ),
        cost_estimate=pl.CostEstimate(
            flops=2_000_000_000, bytes_accessed=5_000_000, transcendentals=800_000
        ),
        name="encode",
    )(*operands)


def solution(mesh):
    placed = (
        P(None, ("grid", "mesh")),
        P(None, ("grid", "mesh")),
        P(("grid", "mesh")),
        P(("grid", "mesh")),
        P(("grid", "mesh")),
        P(("grid", "mesh"), None),
        P(("grid", "mesh")),
        P(),
        P(),
        P(),
        P(),
        P(),
        P(),
        P(),
        P(),
    )
    return jax.shard_map(
        shards, mesh=mesh, in_specs=placed, out_specs=P(("grid", "mesh"), None), check_vma=False
    )
```

time: 135 us -> 33.7 us (0.25)
  the two profiles are of different devices: /device:TPU:4 before, /device:TPU:1 now
where the time goes in v1:
time: 33.7 us; the launch traced here: 33.6 us
  Pallas kernels  32.9 us (98%)
  local copies, waits for them, and re-layouts  0.66 us (2%)
    pallas_call x1, Pallas kernels, shards(): pl.pallas_call(functools.partial(kernel, groups, columns), out_shape=pltp...  32.9 us

profile of v1, /device:TPU:1, one launch (start us, length us, event | category | flops | bytes accessed | tf_op | source)
XLA Modules:
  0.0 33.6 jit_solution(8387345462886683225)
XLA Ops:
  0.0 32.9 %encode.1 = bf16[128,512]{1,0:T(8,128)(2,1)S(1)} custom-call(bf16[474,256]{1,0:T(8,128)(2,1)} %feat_h.1, f32[4,512]{1,0:T(4,128)} %ef_h.1, s32[1,512]{1,0:T(1,128)} %bitcast.5, s32[1,512]{1,0:T(1,128)} %bitcast.6, bf16[128,512]{1,0:T(8,128)(2,1)} %lat_h.1, s32[1,128]{1,0:T(1,128)} %bitcast.9, bf16[474,512]{1,0:T(8,128)(2,1)} %w_grid_h.1, f32[4,512]{1,0:T(4,128)} %w_edge_h.1, ...), custom_call_target="tpu_custom_call" | custom-call | flops 2000000000 | bytes 5000000 | tf_op jit(solution)/shard_map/encode/pallas_call | solution.py:399
  33.0 0.7 %copy.16 = bf16[128,512]{1,0:T(8,128)(2,1)} copy(bf16[128,512]{1,0:T(8,128)(2,1)S(1)} %encode.1) | data formatting | bytes 262144

commit v2 on v1

--- a/solution.py
+++ b/solution.py
@@ -52,6 +52,12 @@
 
 def hot(mask):
     return jnp.where(mask, 1.0, 0.0).astype(BF16)
+
+
+def hot_rows(row, count):
+    at = iota((count, row.shape[1]), 0).astype(F32).astype(BF16)
+    there = jnp.broadcast_to(row.astype(BF16), at.shape)
+    return jnp.where(there == at, jnp.ones_like(at), jnp.zeros_like(at))
 
 
 def parts(v):
@@ -138,7 +144,7 @@
     )
     for at, (here, there) in enumerate(pairs):
         loads[id(there)] = pltpu.make_async_copy(here, there, load_sem.at[at])
-    for there in (dst, omap, src, ef, w_edge, feat, w_grid, w_mi, w_mo, gain_m):
+    for there in (dst, src, ef, w_edge, feat, w_grid, w_mi, w_mo, gain_m):
         loads[id(there)].start()
 
     def ready(*refs):
@@ -186,7 +192,7 @@
 
     shift = (nodes * columns).bit_length() - 1
     upto = hot(iota((slots, slots), 0) <= iota((slots, slots), 1))
-    ready(dst, omap, src, ef, w_edge)
+    ready(dst, src, ef, w_edge, feat, w_grid)
     target = jnp.broadcast_to(dst[...], (8, slots))
     edge_at = iota((8, slots), 1)
     last = jnp.max(jnp.where(target > 0, edge_at, -1), axis=1, keepdims=True)
@@ -202,9 +208,9 @@
     counted = dot(jnp.where(of_owner, fresh_f[0:1], 0.0).astype(BF16), upto)
     rank = jnp.sum(jnp.where(of_owner, counted, 0.0), axis=0, keepdims=True)
     row_of_edge = jnp.where(
-        live[0:1], (rank.astype(jnp.int32) - 1) * groups + owner[0:1], -1
-    )
-    picking = hot(row_of_edge == iota((CAP * groups, slots), 0))
+        live[0:1], (rank - 1.0) * groups + owner[0:1].astype(F32), -1.0
+    )
+    picking = hot_rows(row_of_edge, CAP * groups)
     local_f = jnp.where(fresh, (target & (nodes - 1)).astype(F32), 0.0)
     ids = dot_nt(picking, jnp.broadcast_to(local_f[0:1], (128, slots)).astype(BF16))
     lane = iota((groups, 128), 1)
@@ -213,40 +219,25 @@
         keys = jnp.where(lane & (CAP - 1) == j, ids[j * groups : (j + 1) * groups], keys)
     id_send[...] = keys.reshape(RING, spokes, 1, 128)
 
-    share = nodes // columns
-    node_shift = nodes.bit_length() - 1
-    held = omap[...]
-    home = lax.shift_right_logical(held, node_shift) & (columns - 1)
-    at_home = home == iota((columns, nodes), 0)
-    before = hot(iota((nodes, nodes), 0) <= iota((nodes, nodes), 1))
-    nth = dot(hot(at_home), before)
-    leave = jnp.sum(
-        jnp.where(at_home, nth + (iota((columns, nodes), 0) * share - 1).astype(F32), 0.0),
-        axis=0,
-        keepdims=True,
-    )
-    leaving = hot(leave.astype(jnp.int32) == iota((nodes, nodes), 0))
-    node_hot_t = hot((held & (nodes - 1)) == iota((nodes, nodes), 0))
-    place_send[...] = dot_nt(leaving, node_hot_t).astype(BF16)
-    position = dot_nt(
-        leaving, jnp.broadcast_to(iota((1, nodes), 1).astype(F32), (128, nodes)).astype(BF16)
-    )
-
-    ready(feat, w_grid)
     e1, e2, e3 = parts(ef[...])
     w1, w2, w3 = parts(w_edge[...])
     e_all = jnp.concatenate([e1, e1, e2, e1, e2, e3], axis=0).astype(BF16)
     w_all = jnp.concatenate([w1, w2, w1, w3, w2, w1], axis=0).astype(BF16)
     edge_latent = silu(dot_tn(e_all, w_all)).astype(BF16)
     grid_latent = silu(dot_tn(feat[...], w_grid[...])).astype(BF16)
-    from_node = jnp.transpose(jnp.broadcast_to(src[...], (128, slots)))
-    gathering = [hot(from_node == iota((slots, 128), 1) + at) for at in range(0, g_nodes, 128)]
+    from_node = jnp.transpose(jnp.broadcast_to(src[...], (128, slots)).astype(F32)).astype(BF16)
+    lane_at = iota((slots, 128), 1).astype(F32)
+    one, none = jnp.ones((slots, 128), BF16), jnp.zeros((slots, 128), BF16)
+    gathering = [
+        jnp.where(from_node == (lane_at + float(at)).astype(BF16), one, none)
+        for at in range(0, g_nodes, 128)
+    ]
     ready(w_mi)
     w_mi[width : width + g_nodes] = dot(grid_latent, w_mi[width:]).astype(BF16)
     both = jnp.concatenate([edge_latent] + gathering, axis=1)
     hidden = silu(dot(both, w_mi[0 : width + g_nodes])).astype(BF16)
     ready(w_mo, gain_m)
-    for there in (lat, w_ni, w_no, gain_n):
+    for there in (omap, lat, w_ni, w_no, gain_n):
         loads[id(there)].start()
     mixed = dot(hidden, w_mo[...])
     message[...] = (edge_latent.astype(F32) + normed(mixed) * gain_m[...]).astype(BF16)
@@ -301,9 +292,8 @@
 
     def pay_ring(turn, carry):
         at = ring_turn(turn)
-        for spoke_step in range(spokes):
-            spoke = lax.rem(spoke_at + spoke_step, spokes)
-            peer = (lax.div(spoke, CORES) * RING + at) * CORES + lax.rem(spoke, CORES)
+        for spoke in range(spokes):
+            peer = (spoke // CORES * RING + at) * CORES + spoke % CORES
             block = send.at[at * spokes + spoke]
             remote(block, recv.at[slot], pay_sems, {"grid": peer}).start()
         return carry
@@ -316,6 +306,26 @@
     recv[pl.ds(slot, 1)] = send[pl.ds(ring_at * spokes + spoke_at, 1)]
     drain(id_sems.at[1], id_passed.at[pl.ds(0, RING - 1)])
     along_spokes(id_passed, id_recv, id_sems_2)
+
+    share = nodes // columns
+    node_shift = nodes.bit_length() - 1
+    ready(omap)
+    held = omap[...]
+    home = lax.shift_right_logical(held, node_shift) & (columns - 1)
+    at_home = home == iota((columns, nodes), 0)
+    before = hot(iota((nodes, nodes), 0) <= iota((nodes, nodes), 1))
+    nth = dot(hot(at_home), before)
+    leave = jnp.sum(
+        jnp.where(at_home, nth + (iota((columns, nodes), 0) * share - 1).astype(F32), 0.0),
+        axis=0,
+        keepdims=True,
+    )
+    leaving = hot_rows(leave, nodes)
+    node_hot_t = hot((held & (nodes - 1)) == iota((nodes, nodes), 0))
+    place_send[...] = dot_nt(leaving, node_hot_t).astype(BF16)
+    position = dot_nt(
+        leaving, jnp.broadcast_to(iota((1, nodes), 1).astype(F32), (128, nodes)).astype(BF16)
+    )
 
     along_mesh(place_send, place_recv, place_sems)
 

time: 33.7 us -> 32.7 us (0.970)
  Pallas kernels: 32.9 us -> 31.9 us
    pallas_call x1, Pallas kernels: 32.9 us -> 31.9 us  [shards(): pl.pallas_call(functools.partial(kernel, groups, columns), out_shape=pltp...]
where the time goes in v2:
time: 32.7 us; the launch traced here: 32.6 us
  Pallas kernels  31.9 us (98%)
  local copies, waits for them, and re-layouts  0.66 us (2%)
    pallas_call x1, Pallas kernels, shards(): pl.pallas_call(functools.partial(kernel, groups, columns), out_shape=pltp...  31.9 us
    unnamed x1, local copies, waits for them, and re-layouts  0.66 us

profile of v2, /device:TPU:1, one launch (start us, length us, event | category | flops | bytes accessed | tf_op | source)
XLA Modules:
  0.0 32.6 jit_solution(1211090105910664996)
XLA Ops:
  0.0 31.9 %encode.1 = bf16[128,512]{1,0:T(8,128)(2,1)S(1)} custom-call(bf16[474,256]{1,0:T(8,128)(2,1)} %feat_h.1, f32[4,512]{1,0:T(4,128)} %ef_h.1, s32[1,512]{1,0:T(1,128)} %bitcast.5, s32[1,512]{1,0:T(1,128)} %bitcast.6, bf16[128,512]{1,0:T(8,128)(2,1)} %lat_h.1, s32[1,128]{1,0:T(1,128)} %bitcast.9, bf16[474,512]{1,0:T(8,128)(2,1)} %w_grid_h.1, f32[4,512]{1,0:T(4,128)} %w_edge_h.1, ...), custom_call_target="tpu_custom_call" | custom-call | flops 2000000000 | bytes 5000000 | tf_op jit(solution)/shard_map/encode/pallas_call | solution.py:409
  31.9 0.7 %copy.16 = bf16[128,512]{1,0:T(8,128)(2,1)} copy(bf16[128,512]{1,0:T(8,128)(2,1)S(1)} %encode.1) | data formatting | bytes 262144

commit v3 on v2

--- a/solution.py
+++ b/solution.py
@@ -144,7 +144,7 @@
     )
     for at, (here, there) in enumerate(pairs):
         loads[id(there)] = pltpu.make_async_copy(here, there, load_sem.at[at])
-    for there in (dst, src, ef, w_edge, feat, w_grid, w_mi, w_mo, gain_m):
+    for there in (dst, src, ef, w_edge, feat, w_grid):
         loads[id(there)].start()
 
     def ready(*refs):
@@ -189,6 +189,9 @@
     for step in mesh_steps:
         to = {"mesh": lax.rem(my + step, columns)}
         pl.semaphore_signal(barrier, inc=1, device_id=to, device_id_type=MESH)
+
+    for there in (w_mi, w_mo, gain_m):
+        loads[id(there)].start()
 
     shift = (nodes * columns).bit_length() - 1
     upto = hot(iota((slots, slots), 0) <= iota((slots, slots), 1))
@@ -290,12 +293,18 @@
 
     along_ring(id_send, id_passed, id_sems)
 
+    spoke_order = []
+    for step in [0] + spoke_steps:
+        spoke = lax.rem(spoke_at + step, spokes)
+        first = lax.div(spoke, CORES) * (RING * CORES) + lax.rem(spoke, CORES)
+        spoke_order.append((spoke, first))
+
     def pay_ring(turn, carry):
         at = ring_turn(turn)
-        for spoke in range(spokes):
-            peer = (spoke // CORES * RING + at) * CORES + spoke % CORES
+        for spoke, first in spoke_order:
             block = send.at[at * spokes + spoke]
-            remote(block, recv.at[slot], pay_sems, {"grid": peer}).start()
+            peer = {"grid": first + at * CORES}
+            remote(block, recv.at[slot], pay_sems, peer).start()
         return carry
 
     lax.fori_loop(0, RING - 1, pay_ring, 0)

time: 32.7 us -> 33.5 us (1.024)
  Pallas kernels: 31.9 us -> 32.7 us
    pallas_call x1, Pallas kernels: 31.9 us -> 32.7 us  [shards(): pl.pallas_call(functools.partial(kernel, groups, columns), out_shape=pltp...]
where the time goes in v3:
time: 33.5 us; the launch traced here: 33.3 us
  Pallas kernels  32.7 us (98%)
  local copies, waits for them, and re-layouts  0.66 us (2%)
    pallas_call x1, Pallas kernels, shards(): pl.pallas_call(functools.partial(kernel, groups, columns), out_shape=pltp...  32.7 us

profile of v3, /device:TPU:1, one launch (start us, length us, event | category | flops | bytes accessed | tf_op | source)
XLA Modules:
  0.0 33.3 jit_solution(17408336692226516779)
XLA Ops:
  0.0 32.7 %encode.1 = bf16[128,512]{1,0:T(8,128)(2,1)S(1)} custom-call(bf16[474,256]{1,0:T(8,128)(2,1)} %feat_h.1, f32[4,512]{1,0:T(4,128)} %ef_h.1, s32[1,512]{1,0:T(1,128)} %bitcast.5, s32[1,512]{1,0:T(1,128)} %bitcast.6, bf16[128,512]{1,0:T(8,128)(2,1)} %lat_h.1, s32[1,128]{1,0:T(1,128)} %bitcast.9, bf16[474,512]{1,0:T(8,128)(2,1)} %w_grid_h.1, f32[4,512]{1,0:T(4,128)} %w_edge_h.1, ...), custom_call_target="tpu_custom_call" | custom-call | flops 2000000000 | bytes 5000000 | tf_op jit(solution)/shard_map/encode/pallas_call | solution.py:418
  32.7 0.7 %copy.16 = bf16[128,512]{1,0:T(8,128)(2,1)} copy(bf16[128,512]{1,0:T(8,128)(2,1)S(1)} %encode.1) | data formatting | bytes 262144
